TPU v7x, 32 devices: a whole 2x2x4 slice. The times are simulated.
32 devices in a mesh: grp: 2 (over x), aux: 8 (over z, y), pair: 2 (over core).
Axes of the slice: x: 2, y: 2, z: 4, core: 2. Of those that a mesh axis runs over, the one named last changes fastest.
Arguments:
- integrals: float32 [512, 384, 384], P(('grp', 'aux'), 'pair'), parts along dimension 0, may hold values from -6 to 6
- coef: float32 [384, 256], replicated, may hold values from -0.3125 to 0.3125
- screen: int32 [6, 6], replicated, may hold values 0 or 1
- domains: int32 [256, 128], replicated, may hold values from 0 to 255, all different within a row
- owner: int32 [32768], replicated, may hold values from 0 to 32767, each once
- metric: float32 [512, 256], P(('grp', 'aux'), 'pair'), parts along dimension 0, may hold values from -0.375 to 0.375
Outputs:
- fitted: float32 [512, 32768], P('grp', ('aux', 'pair')), parts along dimension 0
There are 2 independent parts, one for each index of `grp`. A program takes and returns all parts, laid end to end along the dimension named above; an argument that names none is the same for every part. Nothing has to cross between parts.
Inputs may be any that keep to these rules, and one draw needn't show every extreme that they name: `domains`: each row names distinct orbitals and every orbital is named by some row. `owner`: each pair appears once.
All inputs are finite; a program needn't handle non-finite values.
Results may differ from a plain program's by a relative error of at most 0.000071.
Values sent between devices are 32-bit elements; how exact they have to be, the bound alone decides.
A program may use at most 192 MiB of HBM per device.

v0:
```python
import jax
import jax.numpy as jnp
from jax import lax
from jax.sharding import PartitionSpec as P


def body(integrals, coef, screen, domains, owner, metric):
    aux_loc, mu_loc, basis_width = integrals.shape
    occ_count = coef.shape[1]
    block_count = basis_width // 64
    domain_width = domains.shape[1]
    core_count = lax.axis_size("pair")
    core_index = lax.axis_index("pair")
    aux_count = lax.axis_size("aux")
    pair_dev = owner.shape[0] // (aux_count * core_count)
    blocks = screen.astype(jnp.float32)
    row_blocks = jnp.repeat(blocks, 64, axis=0)
    row_mask = lax.dynamic_slice_in_dim(row_blocks, core_index * mu_loc, mu_loc, 0)
    blocked = integrals.reshape(aux_loc, mu_loc, block_count, 64)
    coef_blocked = coef.reshape(block_count, 64, occ_count)
    half_ints = jnp.einsum(
        "pmcn,mc,cni->pmi", blocked, row_mask, coef_blocked, precision=lax.Precision.HIGHEST
    )
    coef_rows = lax.dynamic_slice_in_dim(coef, core_index * mu_loc, mu_loc, 0)
    quarter = jnp.einsum("mi,pmj->pij", coef_rows, half_ints, precision=lax.Precision.HIGHEST)
    occ_first = owner // domain_width
    occ_second = domains[occ_first, owner % domain_width]
    flat_index = occ_first * occ_count + occ_second
    chosen = jnp.take(quarter.reshape(aux_loc, occ_count * occ_count), flat_index, axis=1)
    pieces = chosen.reshape(aux_loc, aux_count, core_count, pair_dev)
    reduced = lax.psum_scatter(pieces, "pair", scatter_dimension=2, tiled=True)
    arrived = lax.all_to_all(reduced, "aux", split_axis=1, concat_axis=0, tiled=True)
    owned = arrived.reshape(aux_loc * aux_count, pair_dev)
    metric_wide = lax.all_gather(metric, "pair", axis=1, tiled=True)
    return jnp.dot(
        lax.all_gather(metric_wide, "aux", axis=0, tiled=True),
        owned,
        precision=lax.Precision.HIGHEST,
        preferred_element_type=jnp.float32,
    )


def solution(mesh):
    placed = (P(("grp", "aux"), "pair", None), P(), P(), P(), P(), P(("grp", "aux"), "pair"))
    return jax.shard_map(
        body, mesh=mesh, in_specs=placed, out_specs=P("grp", ("aux", "pair")), check_vma=False
    )
```

profile of v0, /device:TPU:0, one launch (start us, length us, event | category | flops | bytes accessed | tf_op | source)
XLA Modules:
  0.0 549.0 jit_solution(17488980829703684468)
XLA Ops:
  6.5 0.7 convert_element_type.3
  7.3 0.1 copy.21
  7.4 0.1 broadcast_in_dim.27
  7.5 0.1 reshape.28
  7.5 11.5 %copy.22 = f32[32,192,384]{1,2,0:T(8,128)} copy(f32[32,192,384]{2,1,0:T(8,128)} %param.6) | data formatting | bytes 18874368 | tf_op args[0]
  19.0 0.1 constant_dynamic-slice_fusion.1
  19.1 24.1 %fusion = f32[192,32,256,1]{2,0,3,1:T(8,128)S(1)} fusion(f32[6,64,256,1]{2,1,0,3:T(8,128)S(1)} %bitcast.45, f32[32,192,6,64]{1,3,2,0:T(8,128)} %bitcast.47, f32[192,6]{0,1:T(8,128)S(1)} %constant_dynamic-slice_fusion.1), kind=kOutput, calls=%fused_computation.2 | convolution fusion | flops 7250116608 | bytes 16126464 | tf_op jit(solution)/shard_map/pmcn,mc,cni->pmi/dot_general | solution.py:21
  43.2 16.7 %fusion.6 = f32[32,256,256]{1,2,0:T(8,128)} fusion(f32[192,32,256,1]{2,0,3,1:T(8,128)S(1)} %fusion, f32[384,256]{1,0:T(8,128)S(1)} %copy-done, s32[]{:T(128)S(6)} %select_n.36), kind=kOutput, calls=%fused_computation.8 | convolution fusion | flops 4831838208 | bytes 14876676 | tf_op jit(solution)/shard_map/mi,pmj->pij/dot_general | solution.py:25
  60.0 26.7 %copy.28 = f32[32,256,256]{0,2,1:T(8,128)} copy(f32[32,256,256]{1,2,0:T(8,128)} %fusion.6) | data formatting | bytes 16777216 | tf_op jit(solution)/shard_map/reshape | solution.py:29
  86.7 0.2 fusion.13
  86.9 0.7 copy-done.2
  87.6 201.1 %gather_fusion = s32[32768]{0:T(1024)S(1)} fusion(s32[256,128]{1,0:T(8,128)S(1)} %copy-done.2, s32[32768]{0:T(1024)S(1)} %fusion.13), kind=kCustom, calls=%fused_computation | custom fusion | bytes 524288 | tf_op jit(solution)/shard_map/gather | solution.py:27
  288.7 0.1 compare_and_fusion
  288.9 119.0 %gather_fusion.1 = f32[32768,32]{1,0:T(8,128)} fusion(f32[32,65536]{0,1:T(8,128)} %bitcast.46, s32[32768]{0:T(1024)S(1)} %broadcast_clamp_fusion), kind=kCustom, calls=%fused_computation.1 | custom fusion | bytes 8519680 | tf_op jit(solution)/shard_map/jit(_take)/gather | solution.py:29
  407.9 11.4 %copy.25 = f32[32,8,2,2048]{3,0,2,1:T(8,128)} copy(f32[32,8,2,2048]{0,3,2,1:T(8,128)} %bitcast.48) | data formatting | bytes 8388608 | tf_op jit(solution)/shard_map/jit(_take)/gather | solution.py:29
  419.4 5.0 broadcast_select_fusion
  424.4 0.7 dynamic-slice
  425.1 30.6 %all-reduce.3.cloned.1.call-done = f32[32,8,2,2048]{3,0,2,1:T(8,128)} async-done(((f32[32,8,2,2048]{3,0,2,1:T(8,128)}), f32[32,8,2,2048]{3,0,2,1:T(8,128)}) %all-reduce.3.cloned.1.call-update) | async-done | bytes 4194320
  455.7 3.8 constant_dynamic-slice_fusion
  459.5 5.8 %all-to-all-start = ((f32[32,8,1,2048]{3,0,2,1:T(8,128)}), f32[32,8,1,2048]{3,0,2,1:T(8,128)S(1)}, u32[]{:S(2)}, u32[]{:S(2)}) async-start(f32[32,8,1,2048]{3,0,2,1:T(8,128)} %constant_dynamic-slice_fusion), calls=%async_computation | async-start | bytes 4194304 | tf_op jit(solution)/shard_map/all_to_all | solution.py:32
  465.3 1.8 all_gather.6
  467.1 67.3 %all_gather.7 = f32[256,256]{1,0:T(8,128)S(1)} all-gather(f32[32,256]{1,0:T(8,128)S(1)} %all_gather.6), channel_id=1, replica_groups=mesh['grp'=2,'aux'=8,'pair'=2] {'aux'}, dimensions={0}, use_global_device_ids=true | all-gather | bytes 294912 | tf_op jit(solution)/shard_map/all_gather | solution.py:36
  534.5 4.8 convolution_bitcast_fusion
  539.2 2.9 copy.26
  (16 shorter events, 0.1 us)
Async XLA Ops:
  6.5 12.5 %copy-start = (f32[384,256]{1,0:T(8,128)S(1)}, f32[384,256]{1,0:T(8,128)}, u32[]{:S(2)}) copy-start(f32[384,256]{1,0:T(8,128)} %param.7) | copy-start | bytes 1179652
  6.5 449.2 %all-reduce.3.cloned.1.call-start = ((), (), s32[]{:S(2)}) async-start(), calls=%async_computation.1 | async-start | bytes 8388608
  60.0 26.7 %copy-start.3 = (s32[32768]{0:T(1024)S(1)}, s32[32768]{0:T(1024)}, u32[]{:S(2)}) copy-start(s32[32768]{0:T(1024)} %param.10) | copy-start | bytes 393220
  86.7 0.9 copy-start.2
  419.3 5.1 copy-start.5
  419.4 45.9 %copy-start.4 = (f32[32,128]{1,0:T(8,128)S(1)}, f32[32,128]{1,0:T(8,128)}, u32[]{:S(2)}) copy-start(f32[32,128]{1,0:T(8,128)} %param.11) | copy-start | bytes 49156
  424.4 117.7 %copy-start.1 = (f32[384,256]{1,0:T(8,128)S(1)}, f32[384,256]{1,0:T(8,128)}, u32[]{:S(2)}) copy-start(f32[384,256]{1,0:T(8,128)} %param.7) | copy-start | bytes 1179652
  459.5 74.9 %all-to-all-start = ((f32[32,8,1,2048]{3,0,2,1:T(8,128)}), f32[32,8,1,2048]{3,0,2,1:T(8,128)S(1)}, u32[]{:S(2)}, u32[]{:S(2)}) async-start(f32[32,8,1,2048]{3,0,2,1:T(8,128)} %constant_dynamic-slice_fusion), calls=%async_computation | async-start | bytes 4194304 | tf_op jit(solution)/shard_map/all_to_all | solution.py:32
Sparse Core Ops, SparseCore 0:
  424.5 31.1 all-reduce.2
where the time goes:
time: 550 us; the launch traced here: 549 us
  local copies, waits for them, and re-layouts  378 us (69%)
  blocking collectives  69.2 us (13%)
  matrix products  45.7 us (8%)
  waiting for transfers between devices  30.6 us (6%)
  between operations  13.5 us (2%)
  other arithmetic  6.06 us (1%)
  starting transfers between devices  5.78 us (1%)
    gather x1, local copies, waits for them, and re-layouts, body(): occ_second = domains[occ_first, owner % domain_width]  201 us
    gather x2, local copies, waits for them, and re-layouts, body(): jnp.take(quarter.reshape(aux_loc, occ_count * occ_count), flat_index, axi...  130 us
    all_gather x1, blocking collectives, body(): lax.all_gather(metric_wide, 'aux', axis=0, tiled=True)  67.3 us
    unnamed x2, waiting for transfers between devices  30.6 us
    reshape x1, local copies, waits for them, and re-layouts, body(): quarter.reshape(aux_loc, occ_count * occ_count)  26.7 us
    dot_general x1, matrix products, body(): jnp.einsum('pmcn,mc,cni->pmi', blocked, row_mask, coef_blocked, precision...  24.1 us
    dot_general x1, matrix products, body(): jnp.einsum('mi,pmj->pij', coef_rows, half_ints, precision=lax.Precision.H...  16.7 us
    unnamed x15, local copies, waits for them, and re-layouts  16.7 us
  transfers between devices with their start and end apart: 2, of which 1 were waited for; matrix products, arithmetic and copies ran while one was open for 0% of the time, Pallas kernels for 0%

commit v1 on v0

v1 whole, which is shorter than its diff:
```python
import functools

import jax
import jax.numpy as jnp
from jax import lax
from jax.experimental import pallas as pl
from jax.experimental.pallas import tpu as pltpu
from jax.sharding import PartitionSpec as P

MESH = pl.DeviceIdType.MESH
LANES = 128
VMEM_LIMIT = 60 * 1024 * 1024


def split2(x):
    hi = x.astype(jnp.bfloat16)
    lo = (x - hi.astype(jnp.float32)).astype(jnp.bfloat16)
    return hi, lo


def dot3(a, b, dims=(((1,), (0,)), ((), ()))):
    (ah, al), (bh, bl) = a, b
    mm = functools.partial(lax.dot_general, dimension_numbers=dims, preferred_element_type=jnp.float32)
    return mm(ah, bh) + (mm(ah, bl) + mm(al, bh))


def spread(x, lane):
    quarter = LANES // 4
    group = lane // quarter
    odd = (group % 2) == 1
    high = group >= 2
    even_pair = jnp.where(odd, pltpu.roll(x, quarter, 1), x)
    odd_pair = jnp.where(odd, x, pltpu.roll(x, LANES - quarter, 1))
    even_far = pltpu.roll(even_pair, 2 * quarter, 1)
    odd_far = pltpu.roll(odd_pair, 2 * quarter, 1)
    return (
        jnp.where(high, even_far, even_pair),
        jnp.where(high, odd_far, odd_pair),
        jnp.where(high, even_pair, even_far),
        jnp.where(high, odd_pair, odd_far),
    )


def transform_kernel(
    integrals_ref, mask_ref, coef_ref, coef_t_ref, rows_ref, owner_ref, out_ref,
    ibuf, coef_hl, coef_t_hl, t0, t1, table, sems,
):
    aux_loc, mu_loc, nb = integrals_ref.shape
    nocc = coef_ref.shape[1]
    dests, rows_per, _ = out_ref.shape

    def fetch(p, slot):
        return pltpu.make_async_copy(integrals_ref.at[p], ibuf.at[slot], sems.at[slot])

    fetch(0, 0).start()
    coef_hl[0], coef_hl[1] = split2(coef_ref[...])
    coef_t_hl[0], coef_t_hl[1] = split2(coef_t_ref[...])

    def one_p(p, carry):
        slot = lax.rem(p, 2)

        @pl.when(p + 1 < aux_loc)
        def _():
            fetch(p + 1, 1 - slot).start()

        fetch(p, slot).wait()
        x = split2(ibuf[slot] * mask_ref[...])
        half = split2(dot3(x, (coef_hl[0], coef_hl[1])))
        q = dot3((coef_t_hl[0], coef_t_hl[1]), half)
        t0[pl.ds(p, nocc, stride=aux_loc), :] = q[:, :LANES]
        t1[pl.ds(p, nocc, stride=aux_loc), :] = q[:, LANES:]
        return carry

    lax.fori_loop(0, aux_loc, one_p, 0)

    lane = lax.broadcasted_iota(jnp.int32, (LANES, LANES), 1)

    def one_block(ib, carry):
        for jb, t in enumerate((t0, t1)):
            block = t[pl.ds(pl.multiple_of(ib * LANES, LANES), LANES), :].T
            for g, rep in enumerate(spread(block, lane)):
                at = pl.multiple_of((4 * ib + g) * nocc + jb * LANES, LANES)
                table[pl.ds(at, LANES), :] = rep
        return carry

    lax.fori_loop(0, nocc // 4, one_block, 0)

    row_lane = lax.broadcasted_iota(jnp.int32, (1, LANES), 1) // (LANES // 4)

    for d in range(dests):
        base = d * rows_per * 4

        def eight(rb, carry, d=d, base=base):
            for u in range(8):
                r = rb * 8 + u
                got = [
                    table[pl.ds(rows_ref[owner_ref[base + g * rows_per + r]], 1), :]
                    for g in range(4)
                ]
                low = jnp.where(row_lane == 0, got[0], got[1])
                high = jnp.where(row_lane == 2, got[2], got[3])
                out_ref[d, pl.ds(r, 1), :] = jnp.where(row_lane < 2, low, high)
            return carry

        lax.fori_loop(0, rows_per // 8, eight, 0)


def exchange_kernel(
    n_aux, part_ref, metric_ref, out_ref, pbuf, snd, rcv, mfull,
    psend, precv, asend, arecv, msend, mrecv,
):
    me_a = lax.axis_index("aux")
    me_c = lax.axis_index("pair")
    n_dev = 2 * n_aux
    me = 2 * me_a + me_c
    q_loc = metric_ref.shape[0]
    rows_per = rcv.shape[1]
    barrier = pltpu.get_barrier_semaphore()

    def greet(k, carry):
        to = lax.rem(me + k, n_dev)
        pl.semaphore_signal(barrier, inc=1, device_id={"aux": to // 2, "pair": to % 2}, device_id_type=MESH)
        return carry

    lax.fori_loop(1, n_dev, greet, 0)
    pl.semaphore_wait(barrier, n_dev - 1)

    def pair_copy(t):
        a = lax.rem(me_a + t, n_aux)
        return pltpu.make_async_remote_copy(
            src_ref=part_ref.at[2 * a + (1 - me_c)], dst_ref=pbuf.at[a],
            send_sem=psend.at[t], recv_sem=precv.at[t],
            device_id={"pair": 1 - me_c}, device_id_type=MESH)

    def metric_copy(k, origin):
        to = lax.rem(me + k, n_dev)
        return pltpu.make_async_remote_copy(
            src_ref=metric_ref,
            dst_ref=mfull.at[origin % 2, pl.ds(pl.multiple_of((origin // 2) * q_loc, q_loc), q_loc), :],
            send_sem=msend.at[k], recv_sem=mrecv.at[k],
            device_id={"aux": to // 2, "pair": to % 2}, device_id_type=MESH)

    def aux_copy(t, origin):
        a = lax.rem(me_a + t, n_aux)
        return pltpu.make_async_remote_copy(
            src_ref=snd.at[a], dst_ref=rcv.at[origin],
            send_sem=asend.at[t], recv_sem=arecv.at[t],
            device_id={"aux": a}, device_id_type=MESH)

    def step(f):
        def g(t, carry):
            f(t)
            return carry
        return g

    lax.fori_loop(1, n_aux, step(lambda t: pair_copy(t).start()), 0)
    pair_copy(0).start()

    def send(t):
        pair_copy(t).wait_recv()
        a = lax.rem(me_a + t, n_aux)
        snd[a] = part_ref[2 * a + me_c] + pbuf[a]
        aux_copy(t, me_a).start()

    lax.fori_loop(1, n_aux, step(send), 0)
    lax.fori_loop(1, n_dev, step(lambda k: metric_copy(k, me).start()), 0)
    pair_copy(0).wait_recv()
    rcv[me_a] = part_ref[2 * me_a + me_c] + pbuf[me_a]
    mfull[me_c, pl.ds(pl.multiple_of(me_a * q_loc, q_loc), q_loc), :] = metric_ref[...]

    lax.fori_loop(1, n_dev, step(lambda k: metric_copy(k, lax.rem(me + n_dev - k, n_dev)).wait_recv()), 0)
    lax.fori_loop(1, n_aux, step(lambda t: aux_copy(t, lax.rem(me_a + n_aux - t, n_aux)).wait_recv()), 0)

    quarter = LANES // 4
    lane_group = lax.broadcasted_iota(jnp.int32, (rows_per, LANES), 1) // quarter
    blocks = n_aux // 4
    for g in range(4):
        acc = None
        for b in range(blocks):
            y = None
            for u in range(4):
                x = rcv[4 * b + u]
                shift = (quarter * (u - g)) % LANES
                x = pltpu.roll(x, shift, 1) if shift else x
                y = x if y is None else jnp.where(lane_group == u, x, y)
            per = blocks // 2
            m = mfull_columns(mfull, b, per)
            add = dot3(split2(m), split2(y), (((1,), (1,)), ((), ())))
            acc = add if acc is None else acc + add
        out_ref[:, g * rows_per:(g + 1) * rows_per] = acc

    lax.fori_loop(0, n_aux, step(lambda t: pair_copy(t).wait_send()), 0)
    lax.fori_loop(1, n_aux, step(lambda t: aux_copy(t, me_a).wait_send()), 0)
    lax.fori_loop(1, n_dev, step(lambda k: metric_copy(k, me).wait_send()), 0)


def mfull_columns(mfull, b, per):
    at = (b % per) * LANES
    return mfull[b // per, :, at:at + LANES]


def body(integrals, coef, screen, domains, owner, metric):
    aux_loc, mu_loc, nb = integrals.shape
    nocc = coef.shape[1]
    dom = domains.shape[1]
    core = lax.axis_index("pair")
    n_aux = lax.axis_size("aux")
    dests = 2 * n_aux
    slots = owner.shape[0] // dests
    rows_per = slots // 4
    q_all = metric.shape[0] * n_aux
    block = nb // screen.shape[0]

    kept = jnp.repeat(screen.astype(jnp.float32), block, axis=0)
    kept = lax.dynamic_slice_in_dim(kept, core * mu_loc, mu_loc, 0)
    mask = jnp.repeat(kept, block, axis=1)
    coef_t = lax.dynamic_slice_in_dim(coef, core * mu_loc, mu_loc, 0).T
    rows = (domains + nocc * lax.broadcasted_iota(jnp.int32, domains.shape, 0)).reshape(-1)

    vm = pl.BlockSpec(memory_space=pltpu.VMEM)
    sm = pl.BlockSpec(memory_space=pltpu.SMEM)
    hbm = pl.BlockSpec(memory_space=pl.ANY)
    part = pl.pallas_call(
        transform_kernel,
        out_shape=jax.ShapeDtypeStruct((dests, rows_per, LANES), jnp.float32),
        in_specs=[hbm, vm, vm, vm, sm, sm],
        out_specs=vm,
        scratch_shapes=[
            pltpu.VMEM((2, mu_loc, nb), jnp.float32),
            pltpu.VMEM((2, nb, nocc), jnp.bfloat16),
            pltpu.VMEM((2, nocc, mu_loc), jnp.bfloat16),
            pltpu.VMEM((nocc * aux_loc, LANES), jnp.float32),
            pltpu.VMEM((nocc * aux_loc, LANES), jnp.float32),
            pltpu.VMEM((nocc * nocc, LANES), jnp.float32),
            pltpu.SemaphoreType.DMA((2,)),
        ],
        compiler_params=pltpu.CompilerParams(vmem_limit_bytes=VMEM_LIMIT),
        name="transform",
    )(integrals, mask, coef, coef_t, rows, owner)

    return pl.pallas_call(
        functools.partial(exchange_kernel, n_aux),
        out_shape=jax.ShapeDtypeStruct((q_all, slots), jnp.float32),
        in_specs=[vm, vm],
        out_specs=vm,
        scratch_shapes=[
            pltpu.VMEM((n_aux, rows_per, LANES), jnp.float32),
            pltpu.VMEM((n_aux, rows_per, LANES), jnp.float32),
            pltpu.VMEM((n_aux, rows_per, LANES), jnp.float32),
            pltpu.VMEM((2, q_all, metric.shape[1]), jnp.float32),
            pltpu.SemaphoreType.DMA((n_aux,)),
            pltpu.SemaphoreType.DMA((n_aux,)),
            pltpu.SemaphoreType.DMA((n_aux,)),
            pltpu.SemaphoreType.DMA((n_aux,)),
            pltpu.SemaphoreType.DMA((dests,)),
            pltpu.SemaphoreType.DMA((dests,)),
        ],
        compiler_params=pltpu.CompilerParams(
            vmem_limit_bytes=VMEM_LIMIT, collective_id=0, has_side_effects=True),
        name="exchange",
    )(part, metric)


def solution(mesh):
    placed = (P(("grp", "aux"), "pair", None), P(), P(), P(), P(), P(("grp", "aux"), "pair"))
    return jax.shard_map(
        body, mesh=mesh, in_specs=placed, out_specs=P("grp", ("aux", "pair")), check_vma=False
    )
```

time: 550 us -> 174 us (0.32)
  local copies, waits for them, and re-layouts: 378 us -> 6.11 us
  Pallas kernels: 0 us -> 165 us
  blocking collectives: 69.2 us -> 0 us
  matrix products: 45.7 us -> 0 us
  waiting for transfers between devices: 30.6 us -> 0 us
  between operations: 13.5 us -> 0.03 us
  starting transfers between devices: 5.78 us -> 0 us
    gather x3 -> x0, local copies, waits for them, and re-layouts: 332 us -> none  [the longest x1 201 us: body(): occ_second = domains[occ_first, owner % domain_width]]
    pallas_call x0 -> x2, Pallas kernels: none -> 165 us  [the longest x1 101 us: body(): pl.pallas_call(transform_kernel, out_shape=jax.ShapeDtypeStruct((dests, r...]
    all_gather x2 -> x0, blocking collectives: 69.2 us -> none  [the longest x1 67.3 us: body(): lax.all_gather(metric_wide, 'aux', axis=0, tiled=True)]
    dot_general x3 -> x0, matrix products: 45.7 us -> none  [the longest x1 24.1 us: body(): jnp.einsum('pmcn,mc,cni->pmi', blocked, row_mask, coef_blocked, precision...]
    unnamed x2 -> x0, waiting for transfers between devices: 30.6 us -> none
    reshape x2, local copies, waits for them, and re-layouts: 26.8 us -> 0.94 us  [the longest x1 0.87 us: body(): mask = jnp.repeat(kept, block, axis=1)]
    unnamed x15 -> x2, local copies, waits for them, and re-layouts: 16.7 us -> 3.96 us
    all_to_all x1 -> x0, starting transfers between devices: 5.78 us -> none  [body(): lax.all_to_all(reduced, 'aux', split_axis=1, concat_axis=0, tiled=True)]
  transfers between devices with their start and end apart: 2 -> 0, of which waited for: 1 -> 0; matrix products, arithmetic and copies ran while one was open for 0% -> 0% of each run, Pallas kernels for 0% -> 0%
where the time goes in v1:
time: 174 us
  Pallas kernels  165 us (95%)
  local copies, waits for them, and re-layouts  6.11 us (4%)
  other arithmetic  2.35 us (1%)
    pallas_call x1, Pallas kernels, body(): pl.pallas_call(transform_kernel, out_shape=jax.ShapeDtypeStruct((dests, r...  101 us
    pallas_call x1, Pallas kernels, body(): pl.pallas_call(functools.partial(exchange_kernel, n_aux), out_shape=jax.S...  64 us
    unnamed x2, local copies, waits for them, and re-layouts  3.96 us

profile of v1, /device:TPU:0, one launch (start us, length us, event | category | flops | bytes accessed | tf_op | source)
XLA Modules:
  0.0 173.6 jit_solution(5376532452714433331)
XLA Ops:
  0.0 0.7 convert_element_type.3
  0.7 0.1 copy.8
  0.8 0.1 broadcast_in_dim.6
  0.9 0.1 reshape.9
  0.9 0.1 constant_dynamic-slice_fusion.1
  1.0 1.7 add_bitcast_fusion.rows_ref
  2.7 0.9 constant_dynamic-slice_fusion
  3.6 0.8 copy.11
  4.5 0.9 copy.10.mask_ref
  5.3 101.1 %transform.1.part_ref = f32[16,512,128]{2,1,0:T(8,128)} custom-call(f32[32,192,384]{2,1,0:T(8,128)} %integrals_ref.1, f32[192,384]{1,0:T(8,128)} %copy.10.mask_ref, f32[384,256]{1,0:T(8,128)} %coef_ref.1, f32[256,192]{1,0:T(8,128)} %bitcast.7, s32[32768]{0:T(1024)} %add_bitcast_fusion.rows_ref, s32[32768]{0:T(1024)} %owner_ref.1), custom_call_target="tpu_custom_call" | custom-call | tf_op jit(solution)/shard_map/transform/pallas_call | solution.py:223
  106.5 64.0 %exchange.1 = f32[256,2048]{1,0:T(8,128)} custom-call(f32[16,512,128]{2,1,0:T(8,128)} %transform.1.part_ref, f32[32,128]{1,0:T(8,128)} %metric_ref.1), custom_call_target="tpu_custom_call" | custom-call | tf_op jit(solution)/shard_map/exchange/pallas_call | solution.py:241
  170.5 3.1 %copy.13 = f32[256,2048]{1,0:T(8,128)} copy(f32[256,2048]{1,0:T(8,128)} %exchange.1) | data formatting | bytes 4194304
  (2 shorter events, 0.0 us)

commit v2 on v1

v2 whole, which is shorter than its diff:
```python
import functools

import jax
import jax.numpy as jnp
from jax import lax
from jax.experimental import pallas as pl
from jax.experimental.pallas import tpu as pltpu
from jax.sharding import PartitionSpec as P

MESH = pl.DeviceIdType.MESH
LANES = 128
BATCH = 4
VMEM_LIMIT = 62 * 1024 * 1024


def split2(x):
    hi = x.astype(jnp.bfloat16)
    lo = (x - hi.astype(jnp.float32)).astype(jnp.bfloat16)
    return hi, lo


def dot3(a, b, dims=(((1,), (0,)), ((), ()))):
    (ah, al), (bh, bl) = a, b
    mm = functools.partial(lax.dot_general, dimension_numbers=dims, preferred_element_type=jnp.float32)
    return mm(ah, bh) + (mm(ah, bl) + mm(al, bh))


def spread(x, lane):
    quarter = LANES // 4
    group = lane // quarter
    odd = (group % 2) == 1
    high = group >= 2
    even_pair = jnp.where(odd, pltpu.roll(x, quarter, 1), x)
    odd_pair = jnp.where(odd, x, pltpu.roll(x, LANES - quarter, 1))
    even_far = pltpu.roll(even_pair, 2 * quarter, 1)
    odd_far = pltpu.roll(odd_pair, 2 * quarter, 1)
    return (
        jnp.where(high, even_far, even_pair),
        jnp.where(high, odd_far, odd_pair),
        jnp.where(high, even_pair, even_far),
        jnp.where(high, odd_pair, odd_far),
    )


def fused_kernel(
    n_aux, integrals_ref, screen_ref, coef_ref, rows_ref, owner_ref, metric_ref, out_ref,
    ibuf, mask, coef_hl, coef_t_hl, t0, t1, table, pairs, pbuf, snd, rcv, mfull,
    sems, psend, precv, asend, arecv, msend, mrecv,
):
    aux_loc, mu_loc, nb = integrals_ref.shape
    nocc = coef_ref.shape[1]
    batch = ibuf.shape[1]
    q_loc = metric_ref.shape[0]
    rows_per = rcv.shape[1]
    n_dev = 2 * n_aux
    me_a = lax.axis_index("aux")
    me_c = lax.axis_index("pair")
    me = 2 * me_a + me_c
    quarter = LANES // 4

    def step(f):
        def g(t, carry):
            f(t)
            return carry
        return g

    barrier = pltpu.get_barrier_semaphore()

    def greet(k):
        to = lax.rem(me + k, n_dev)
        pl.semaphore_signal(barrier, inc=1, device_id={"aux": to // 2, "pair": to % 2}, device_id_type=MESH)

    lax.fori_loop(1, n_dev, step(greet), 0)

    def fetch(p, slot):
        return pltpu.make_async_copy(integrals_ref.at[pl.ds(p * batch, batch)], ibuf.at[slot], sems.at[slot])

    fetch(0, 0).start()
    coef_hl[0], coef_hl[1] = split2(coef_ref[...])
    coef_t = coef_ref[pl.ds(pl.multiple_of(me_c * mu_loc, 64), mu_loc), :].T
    coef_t_hl[0], coef_t_hl[1] = split2(coef_t)
    n_blk = screen_ref.shape[0]
    width = nb // n_blk
    lane_blk = lax.broadcasted_iota(jnp.int32, (width, nb), 1) // width
    for rb in range(mu_loc // width):
        line = jnp.zeros((width, nb), jnp.float32)
        for cb in range(n_blk):
            kept = screen_ref[me_c * (mu_loc // width) + rb, cb].astype(jnp.float32)
            line = jnp.where(lane_blk == cb, kept, line)
        mask[rb * width:(rb + 1) * width, :] = line

    n_steps = aux_loc // batch

    def one_step(p, carry):
        slot = lax.rem(p, 2)

        @pl.when(p + 1 < n_steps)
        def _():
            fetch(p + 1, 1 - slot).start()

        fetch(p, slot).wait()
        x = split2((ibuf[slot] * mask[...][None]).reshape(batch * mu_loc, nb))
        hh, hl = split2(dot3(x, (coef_hl[0], coef_hl[1])))
        for u in range(batch):
            at = slice(u * mu_loc, (u + 1) * mu_loc)
            q = dot3((coef_t_hl[0], coef_t_hl[1]), (hh[at], hl[at]))
            t0[pl.ds(p * batch + u, nocc, stride=aux_loc), :] = q[:, :LANES]
            t1[pl.ds(p * batch + u, nocc, stride=aux_loc), :] = q[:, LANES:]
        return carry

    lax.fori_loop(0, n_steps, one_step, 0)

    lane = lax.broadcasted_iota(jnp.int32, (LANES, LANES), 1)

    def one_block(ib):
        for jb, t in enumerate((t0, t1)):
            block = t[pl.ds(pl.multiple_of(ib * LANES, LANES), LANES), :].T
            for g, rep in enumerate(spread(block, lane)):
                at = pl.multiple_of((4 * ib + g) * nocc + jb * LANES, LANES)
                table[pl.ds(at, LANES), :] = rep

    lax.fori_loop(0, nocc // 4, step(one_block), 0)

    row_lane = lax.broadcasted_iota(jnp.int32, (1, LANES), 1) // quarter

    def gather(core, a, out):
        base = (2 * a + core) * (rows_per * 4)

        def some(rb):
            for u in range(16):
                r = rb * 16 + u
                got = [
                    table[pl.ds(rows_ref[owner_ref[base + g * rows_per + r]], 1), :]
                    for g in range(4)
                ]
                low = jnp.where(row_lane == 0, got[0], got[1])
                high = jnp.where(row_lane == 2, got[2], got[3])
                out[a, pl.ds(r, 1), :] = jnp.where(row_lane < 2, low, high)

        lax.fori_loop(0, rows_per // 16, step(some), 0)

    def pair_copy(t):
        a = me_a ^ t
        return pltpu.make_async_remote_copy(
            src_ref=pairs.at[a], dst_ref=pbuf.at[a],
            send_sem=psend.at[t], recv_sem=precv.at[t],
            device_id={"pair": 1 - me_c}, device_id_type=MESH)

    def metric_copy(k, origin):
        to = lax.rem(me + k, n_dev)
        return pltpu.make_async_remote_copy(
            src_ref=metric_ref,
            dst_ref=mfull.at[origin % 2, pl.ds(pl.multiple_of((origin // 2) * q_loc, q_loc), q_loc), :],
            send_sem=msend.at[k], recv_sem=mrecv.at[k],
            device_id={"aux": to // 2, "pair": to % 2}, device_id_type=MESH)

    def aux_copy(t, origin):
        return pltpu.make_async_remote_copy(
            src_ref=snd.at[me_a ^ t], dst_ref=rcv.at[origin],
            send_sem=asend.at[t], recv_sem=arecv.at[t],
            device_id={"aux": me_a ^ t}, device_id_type=MESH)

    pl.semaphore_wait(barrier, n_dev - 1)

    def send(s):
        t = n_aux - 1 - s
        a = me_a ^ t
        gather(1 - me_c, a, pairs)
        pair_copy(t).start()
        gather(me_c, a, snd)
        pair_copy(t).wait_recv()
        snd[a] += pbuf[a]
        aux_copy(t, me_a).start()

    lax.fori_loop(0, n_aux - 1, step(send), 0)
    lax.fori_loop(1, n_dev, step(lambda k: metric_copy(k, me).start()), 0)
    mfull[me_c, pl.ds(pl.multiple_of(me_a * q_loc, q_loc), q_loc), :] = metric_ref[...]
    gather(1 - me_c, me_a, pairs)
    pair_copy(0).start()
    gather(me_c, me_a, snd)
    pair_copy(0).wait_recv()
    rcv[me_a] = snd[me_a] + pbuf[me_a]

    lax.fori_loop(1, n_dev, step(lambda k: metric_copy(k, lax.rem(me + n_dev - k, n_dev)).wait_recv()), 0)

    lane_group = lax.broadcasted_iota(jnp.int32, (rows_per, LANES), 1) // quarter
    blocks = n_aux // 4
    per = blocks // 2
    for s in range(blocks):
        for t in range(4 * s, 4 * s + 4):
            if t > 0:
                aux_copy(t, me_a ^ t).wait_recv()
        b = (me_a // 4) ^ s
        m = split2(mfull[b // per, :, pl.ds(pl.multiple_of((b % per) * LANES, LANES), LANES)])
        for g in range(4):
            y = None
            for u in range(4):
                x = rcv[4 * b + u]
                shift = (quarter * (u - g)) % LANES
                x = pltpu.roll(x, shift, 1) if shift else x
                y = x if y is None else jnp.where(lane_group == u, x, y)
            add = dot3(m, split2(y), (((1,), (1,)), ((), ())))
            if s == 0:
                out_ref[:, g * rows_per:(g + 1) * rows_per] = add
            else:
                out_ref[:, g * rows_per:(g + 1) * rows_per] += add

    lax.fori_loop(0, n_aux, step(lambda t: pair_copy(t).wait_send()), 0)
    lax.fori_loop(1, n_aux, step(lambda t: aux_copy(t, me_a).wait_send()), 0)
    lax.fori_loop(1, n_dev, step(lambda k: metric_copy(k, me).wait_send()), 0)


def body(integrals, coef, screen, domains, owner, metric):
    aux_loc, mu_loc, nb = integrals.shape
    nocc = coef.shape[1]
    n_aux = lax.axis_size("aux")
    dests = 2 * n_aux
    slots = owner.shape[0] // dests
    rows_per = slots // 4
    q_all = metric.shape[0] * n_aux
    rows = (domains + nocc * lax.broadcasted_iota(jnp.int32, domains.shape, 0)).reshape(-1)

    vm = pl.BlockSpec(memory_space=pltpu.VMEM)
    sm = pl.BlockSpec(memory_space=pltpu.SMEM)
    hbm = pl.BlockSpec(memory_space=pl.ANY)
    chunk = pltpu.VMEM((n_aux, rows_per, LANES), jnp.float32)
    half_table = pltpu.VMEM((nocc * aux_loc, LANES), jnp.float32)
    return pl.pallas_call(
        functools.partial(fused_kernel, n_aux),
        out_shape=jax.ShapeDtypeStruct((q_all, slots), jnp.float32),
        in_specs=[hbm, sm, vm, sm, sm, vm],
        out_specs=vm,
        scratch_shapes=[
            pltpu.VMEM((2, BATCH, mu_loc, nb), jnp.float32),
            pltpu.VMEM((mu_loc, nb), jnp.float32),
            pltpu.VMEM((2, nb, nocc), jnp.bfloat16),
            pltpu.VMEM((2, nocc, mu_loc), jnp.bfloat16),
            half_table,
            half_table,
            pltpu.VMEM((nocc * nocc, LANES), jnp.float32),
            chunk,
            chunk,
            chunk,
            chunk,
            pltpu.VMEM((2, q_all, metric.shape[1]), jnp.float32),
            pltpu.SemaphoreType.DMA((2,)),
            pltpu.SemaphoreType.DMA((n_aux,)),
            pltpu.SemaphoreType.DMA((n_aux,)),
            pltpu.SemaphoreType.DMA((n_aux,)),
            pltpu.SemaphoreType.DMA((n_aux,)),
            pltpu.SemaphoreType.DMA((dests,)),
            pltpu.SemaphoreType.DMA((dests,)),
        ],
        compiler_params=pltpu.CompilerParams(
            vmem_limit_bytes=VMEM_LIMIT, collective_id=0, has_side_effects=True),
        name="pair_fit",
    )(integrals, screen, coef, rows, owner, metric)


def solution(mesh):
    placed = (P(("grp", "aux"), "pair", None), P(), P(), P(), P(), P(("grp", "aux"), "pair"))
    return jax.shard_map(
        body, mesh=mesh, in_specs=placed, out_specs=P("grp", ("aux", "pair")), check_vma=False
    )
```

time: 174 us -> 120 us (0.69)
  Pallas kernels: 165 us -> 115 us
  local copies, waits for them, and re-layouts: 6.11 us -> 3.14 us
    pallas_call x2 -> x1, Pallas kernels: 165 us -> 115 us  [body(): pl.pallas_call(functools.partial(fused_kernel, n_aux), out_shape=jax.Shap...]
    unnamed x2 -> x1, local copies, waits for them, and re-layouts: 3.96 us -> 3.14 us
where the time goes in v2:
time: 120 us; the launch traced here: 119 us
  Pallas kernels  115 us (96%)
  local copies, waits for them, and re-layouts  3.14 us (3%)
  other arithmetic  1.66 us (1%)
    pallas_call x1, Pallas kernels, body(): pl.pallas_call(functools.partial(fused_kernel, n_aux), out_shape=jax.Shap...  115 us
    unnamed x1, local copies, waits for them, and re-layouts  3.14 us

profile of v2, /device:TPU:0, one launch (start us, length us, event | category | flops | bytes accessed | tf_op | source)
XLA Modules:
  0.0 119.4 jit_solution(15390310421358438274)
XLA Ops:
  0.0 1.7 %add_bitcast_fusion.rows_ref = s32[32768]{0:T(1024)} fusion(s32[256,128]{1,0:T(8,128)} %param.9, s32[256]{0:T(256)S(1)} %iota_multiply_fusion), kind=kLoop, calls=%fused_computation | loop fusion | flops 32768 | bytes 263168 | tf_op jit(solution)/shard_map/reshape | solution.py:221
  1.7 114.6 %pair_fit.1 = f32[256,2048]{1,0:T(8,128)} custom-call(f32[32,192,384]{2,1,0:T(8,128)} %integrals_ref.1, s32[6,6]{1,0:T(8,128)} %screen_ref.1, f32[384,256]{1,0:T(8,128)} %coef_ref.1, s32[32768]{0:T(1024)} %add_bitcast_fusion.rows_ref, s32[32768]{0:T(1024)} %owner_ref.1, f32[32,128]{1,0:T(8,128)} %metric_ref.1), custom_call_target="tpu_custom_call" | custom-call | tf_op jit(solution)/shard_map/pair_fit/pallas_call | solution.py:228
  116.3 3.1 %copy.8 = f32[256,2048]{1,0:T(8,128)} copy(f32[256,2048]{1,0:T(8,128)} %pair_fit.1) | data formatting | bytes 4194304
  (1 shorter events, 0.0 us)

commit v3 on v2

--- a/solution.py
+++ b/solution.py
@@ -23,23 +23,6 @@
     (ah, al), (bh, bl) = a, b
     mm = functools.partial(lax.dot_general, dimension_numbers=dims, preferred_element_type=jnp.float32)
     return mm(ah, bh) + (mm(ah, bl) + mm(al, bh))
-
-
-def spread(x, lane):
-    quarter = LANES // 4
-    group = lane // quarter
-    odd = (group % 2) == 1
-    high = group >= 2
-    even_pair = jnp.where(odd, pltpu.roll(x, quarter, 1), x)
-    odd_pair = jnp.where(odd, x, pltpu.roll(x, LANES - quarter, 1))
-    even_far = pltpu.roll(even_pair, 2 * quarter, 1)
-    odd_far = pltpu.roll(odd_pair, 2 * quarter, 1)
-    return (
-        jnp.where(high, even_far, even_pair),
-        jnp.where(high, odd_far, odd_pair),
-        jnp.where(high, even_pair, even_far),
-        jnp.where(high, odd_pair, odd_far),
-    )
 
 
 def fused_kernel(
@@ -57,6 +40,7 @@
     me_c = lax.axis_index("pair")
     me = 2 * me_a + me_c
     quarter = LANES // 4
+    pitch = t0.shape[0] // nocc
 
     def step(f):
         def g(t, carry):
@@ -104,18 +88,17 @@
         for u in range(batch):
             at = slice(u * mu_loc, (u + 1) * mu_loc)
             q = dot3((coef_t_hl[0], coef_t_hl[1]), (hh[at], hl[at]))
-            t0[pl.ds(p * batch + u, nocc, stride=aux_loc), :] = q[:, :LANES]
-            t1[pl.ds(p * batch + u, nocc, stride=aux_loc), :] = q[:, LANES:]
+            t0[pl.ds(p * batch + u, nocc, stride=pitch), :] = q[:, :LANES]
+            t1[pl.ds(p * batch + u, nocc, stride=pitch), :] = q[:, LANES:]
         return carry
 
     lax.fori_loop(0, n_steps, one_step, 0)
-
-    lane = lax.broadcasted_iota(jnp.int32, (LANES, LANES), 1)
 
     def one_block(ib):
         for jb, t in enumerate((t0, t1)):
-            block = t[pl.ds(pl.multiple_of(ib * LANES, LANES), LANES), :].T
-            for g, rep in enumerate(spread(block, lane)):
+            for g in range(4):
+                block = t[pl.ds(pl.multiple_of((4 * ib + g) * pitch, 8), aux_loc), :]
+                rep = jnp.concatenate([block] * 4, axis=0).T
                 at = pl.multiple_of((4 * ib + g) * nocc + jb * LANES, LANES)
                 table[pl.ds(at, LANES), :] = rep
 
@@ -224,7 +207,7 @@
     sm = pl.BlockSpec(memory_space=pltpu.SMEM)
     hbm = pl.BlockSpec(memory_space=pl.ANY)
     chunk = pltpu.VMEM((n_aux, rows_per, LANES), jnp.float32)
-    half_table = pltpu.VMEM((nocc * aux_loc, LANES), jnp.float32)
+    half_table = pltpu.VMEM((nocc * (aux_loc + 8), LANES), jnp.float32)
     return pl.pallas_call(
         functools.partial(fused_kernel, n_aux),
         out_shape=jax.ShapeDtypeStruct((q_all, slots), jnp.float32),

time: 120 us -> 107 us (0.89)
  Pallas kernels: 115 us -> 102 us
    pallas_call x1, Pallas kernels: 115 us -> 102 us  [body(): pl.pallas_call(functools.partial(fused_kernel, n_aux), out_shape=jax.Shap...]
where the time goes in v3:
time: 107 us
  Pallas kernels  102 us (95%)
  local copies, waits for them, and re-layouts  3.14 us (3%)
  other arithmetic  1.66 us (2%)
    pallas_call x1, Pallas kernels, body(): pl.pallas_call(functools.partial(fused_kernel, n_aux), out_shape=jax.Shap...  102 us
    unnamed x1, local copies, waits for them, and re-layouts  3.14 us

profile of v3, /device:TPU:0, one launch (start us, length us, event | category | flops | bytes accessed | tf_op | source)
XLA Modules:
  0.0 106.8 jit_solution(8985880432485197734)
XLA Ops:
  0.0 1.7 %add_bitcast_fusion.rows_ref = s32[32768]{0:T(1024)} fusion(s32[256,128]{1,0:T(8,128)} %param.9, s32[256]{0:T(256)S(1)} %iota_multiply_fusion), kind=kLoop, calls=%fused_computation | loop fusion | flops 32768 | bytes 263168 | tf_op jit(solution)/shard_map/reshape | solution.py:204
  1.7 102.0 %pair_fit.1 = f32[256,2048]{1,0:T(8,128)} custom-call(f32[32,192,384]{2,1,0:T(8,128)} %integrals_ref.1, s32[6,6]{1,0:T(8,128)} %screen_ref.1, f32[384,256]{1,0:T(8,128)} %coef_ref.1, s32[32768]{0:T(1024)} %add_bitcast_fusion.rows_ref, s32[32768]{0:T(1024)} %owner_ref.1, f32[32,128]{1,0:T(8,128)} %metric_ref.1), custom_call_target="tpu_custom_call" | custom-call | tf_op jit(solution)/shard_map/pair_fit/pallas_call | solution.py:211
  103.7 3.1 %copy.8 = f32[256,2048]{1,0:T(8,128)} copy(f32[256,2048]{1,0:T(8,128)} %pair_fit.1) | data formatting | bytes 4194304
  (1 shorter events, 0.0 us)

commit v4 on v3

--- a/solution.py
+++ b/solution.py
@@ -144,9 +144,10 @@
             device_id={"aux": me_a ^ t}, device_id_type=MESH)
 
     pl.semaphore_wait(barrier, n_dev - 1)
+    lax.fori_loop(1, n_dev, step(lambda k: metric_copy(k, me).start()), 0)
 
     def send(s):
-        t = n_aux - 1 - s
+        t = (n_aux // 2 + s) % n_aux + s // (n_aux // 2)
         a = me_a ^ t
         gather(1 - me_c, a, pairs)
         pair_copy(t).start()
@@ -156,7 +157,6 @@
         aux_copy(t, me_a).start()
 
     lax.fori_loop(0, n_aux - 1, step(send), 0)
-    lax.fori_loop(1, n_dev, step(lambda k: metric_copy(k, me).start()), 0)
     mfull[me_c, pl.ds(pl.multiple_of(me_a * q_loc, q_loc), q_loc), :] = metric_ref[...]
     gather(1 - me_c, me_a, pairs)
     pair_copy(0).start()

time: 107 us -> 101 us (0.944)
  Pallas kernels: 102 us -> 96 us
    pallas_call x1, Pallas kernels: 102 us -> 96 us  [body(): pl.pallas_call(functools.partial(fused_kernel, n_aux), out_shape=jax.Shap...]
where the time goes in v4:
time: 101 us
  Pallas kernels  96 us (95%)
  local copies, waits for them, and re-layouts  3.14 us (3%)
  other arithmetic  1.66 us (2%)
    pallas_call x1, Pallas kernels, body(): pl.pallas_call(functools.partial(fused_kernel, n_aux), out_shape=jax.Shap...  96 us
    unnamed x1, local copies, waits for them, and re-layouts  3.14 us

profile of v4, /device:TPU:0, one launch (start us, length us, event | category | flops | bytes accessed | tf_op | source)
XLA Modules:
  0.0 100.8 jit_solution(13101168986664669019)
XLA Ops:
  0.0 1.7 %add_bitcast_fusion.rows_ref = s32[32768]{0:T(1024)} fusion(s32[256,128]{1,0:T(8,128)} %param.9, s32[256]{0:T(256)S(1)} %iota_multiply_fusion), kind=kLoop, calls=%fused_computation | loop fusion | flops 32768 | bytes 263168 | tf_op jit(solution)/shard_map/reshape | solution.py:204
  1.7 96.0 %pair_fit.1 = f32[256,2048]{1,0:T(8,128)} custom-call(f32[32,192,384]{2,1,0:T(8,128)} %integrals_ref.1, s32[6,6]{1,0:T(8,128)} %screen_ref.1, f32[384,256]{1,0:T(8,128)} %coef_ref.1, s32[32768]{0:T(1024)} %add_bitcast_fusion.rows_ref, s32[32768]{0:T(1024)} %owner_ref.1, f32[32,128]{1,0:T(8,128)} %metric_ref.1), custom_call_target="tpu_custom_call" | custom-call | tf_op jit(solution)/shard_map/pair_fit/pallas_call | solution.py:211
  97.7 3.1 %copy.8 = f32[256,2048]{1,0:T(8,128)} copy(f32[256,2048]{1,0:T(8,128)} %pair_fit.1) | data formatting | bytes 4194304
  (1 shorter events, 0.0 us)
